TPU v7x, 32 devices: a whole 2x2x4 slice. The times are simulated.
32 devices in a mesh: parts: 1, uly: 8 (over z, x), blk: 4 (over y, core).
Axes of the slice: x: 2, y: 2, z: 4, core: 2. Of those that a mesh axis runs over, the one named last changes fastest.
Arguments:
- queries: bfloat16 [4, 512, 8192], P(('parts', 'blk'), 'uly'), may hold values from -4.5 to 4.5
- keys: bfloat16 [4, 512, 1024], P(('parts', 'blk'), 'uly'), may hold values from -4.5 to 4.5
- values: bfloat16 [4, 512, 1024], P(('parts', 'blk'), 'uly'), may hold values from -6 to 6
- doc_blocks: int32 [4], P('parts'), may hold values from 1 to 12, 16 in all
Outputs:
- attended: bfloat16 [4, 512, 8192], P(('parts', 'blk'), 'uly')
Inputs may be any that keep to these rules, and one draw needn't show every extreme that they name: `doc_blocks`: the lengths sum to 16; the longest document holds exactly (3) * 512 tokens.
All inputs are finite; a program needn't handle non-finite values.
Results may differ from a plain program's by a relative error of at most 0.0037.
Values may be sent and summed in bfloat16 or wider, within the bound.
A program may use at most 128 MiB of HBM per device.

v0:
```python
import jax
import jax.numpy as jnp
from jax import lax
from jax.sharding import PartitionSpec as P

HEAD_WIDTH = 128
BLOCK = 128


def segment_of(positions, ends):
    return jnp.sum((positions[:, None] >= ends[None, :]).astype(jnp.int32), axis=1)


def on_device(queries, keys, values, doc_blocks):
    moved_q, moved_k, moved_v = (
        lax.all_to_all(queries, "uly", split_axis=2, concat_axis=1, tiled=True),
        lax.all_to_all(keys, "uly", split_axis=2, concat_axis=1, tiled=True),
        lax.all_to_all(values, "uly", split_axis=2, concat_axis=1, tiled=True),
    )
    slot = moved_q.shape[1]
    local_q = moved_q.shape[2] // HEAD_WIDTH
    local_kv = moved_k.shape[2] // HEAD_WIDTH
    query_group = local_q // local_kv
    scale = HEAD_WIDTH ** (-0.5)
    first_index = lax.axis_index("blk") * slot
    ends = jnp.cumsum(doc_blocks) * BLOCK
    qpos = first_index + jnp.arange(slot, dtype=jnp.int32)
    qseg = segment_of(qpos, ends)
    qheads = jnp.transpose(moved_q[0].reshape(slot, local_q, HEAD_WIDTH), (1, 0, 2))
    stacked = jnp.concatenate([moved_k, moved_v], axis=0)

    def allowed_for(kpos):
        kseg = segment_of(kpos, ends)
        return (qseg[:, None] == kseg[None, :]) & (kpos[None, :] <= qpos[:, None])

    start_state = (
        jnp.full((local_q, slot), -1e30, jnp.float32),
        jnp.zeros((local_q, slot), jnp.float32),
        jnp.zeros((local_q, slot, HEAD_WIDTH), jnp.float32),
    )
    piece = lax.all_gather(stacked, "blk", axis=1, tiled=True)
    start = jnp.int32(0)
    count = piece.shape[1]

    def work(state):
        key_piece = piece[0].reshape(count, local_kv, HEAD_WIDTH)
        value_piece = piece[1].reshape(count, local_kv, HEAD_WIDTH)
        allowed = allowed_for(jnp.arange(count, dtype=jnp.int32))

        def one_head(inputs):
            head, running, summed, accum = inputs
            qh = lax.dynamic_index_in_dim(qheads, head, 0, keepdims=False)
            kh = lax.dynamic_index_in_dim(key_piece, head // query_group, 1, keepdims=False)
            vh = lax.dynamic_index_in_dim(value_piece, head // query_group, 1, keepdims=False)
            scores = jnp.dot(qh, kh.T, preferred_element_type=jnp.float32) * scale
            scores = jnp.where(allowed, scores, -1e30)
            newest = jnp.maximum(running, jnp.max(scores, axis=1))
            expo = jnp.where(allowed, jnp.exp(scores - newest[:, None]), 0.0)
            factor = jnp.exp(running - newest)
            summed = summed * factor + jnp.sum(expo, axis=1)
            accum = accum * factor[:, None] + jnp.dot(
                expo.astype(jnp.bfloat16), vh, preferred_element_type=jnp.float32
            )
            return (newest, summed, accum)

        return lax.map(one_head, (jnp.arange(local_q, dtype=jnp.int32),) + tuple(state))

    last_seg = jnp.sum((start + count - 1 >= ends).astype(jnp.int32))
    useful = (start < first_index + slot) & (last_seg >= qseg[0])
    running, summed, accum = lax.cond(useful, work, lambda state: state, start_state)
    heads = (accum / summed[:, :, None]).astype(jnp.bfloat16)
    outputs = jnp.transpose(heads, (1, 0, 2)).reshape(1, slot, local_q * HEAD_WIDTH)
    return lax.all_to_all(outputs, "uly", split_axis=1, concat_axis=2, tiled=True)


def solution(mesh):
    return jax.shard_map(
        on_device,
        mesh=mesh,
        in_specs=(
            P(("parts", "blk"), "uly", None),
            P(("parts", "blk"), "uly", None),
            P(("parts", "blk"), "uly", None),
            P("parts"),
        ),
        out_specs=P(("parts", "blk"), "uly", None),
        check_vma=False,
    )
```

profile of v0, /device:TPU:0, one launch (start us, length us, event | category | flops | bytes accessed | tf_op | source)
XLA Modules:
  0.0 288.8 jit_solution(3122139302436172194)
XLA Ops:
  8.4 2.3 reduce
  11.6 7.3 %all-to-all-start.1 = ((bf16[8,2,4096]{2,1,0:T(2,128)(2,1)}), bf16[8,2,4096]{2,1,0:T(2,128)(2,1)S(1)}, u32[]{:S(2)}, u32[]{:S(2)}) async-start(bf16[8,2,4096]{2,1,0:T(2,128)(2,1)} %reshape.75), calls=%async_computation.1 | async-start | bytes 262144 | tf_op jit(solution)/shard_map/all_to_all | solution.py:18
  20.1 2.3 reduce.1
  23.3 2.9 %all-to-all-done.1 = bf16[8,2,4096]{2,1,0:T(2,128)(2,1)S(1)} async-done(((bf16[8,2,4096]{2,1,0:T(2,128)(2,1)}), bf16[8,2,4096]{2,1,0:T(2,128)(2,1)S(1)}, u32[]{:S(2)}, u32[]{:S(2)}) %all-to-all-start.1) | async-done | bytes 131104 | tf_op jit(solution)/shard_map/all_to_all | solution.py:18
  26.2 3.4 %all-to-all-start = ((bf16[8,2,4096]{2,1,0:T(2,128)(2,1)}), bf16[8,2,4096]{2,1,0:T(2,128)(2,1)S(1)}, u32[]{:S(2)}, u32[]{:S(2)}) async-start(bf16[8,2,4096]{2,1,0:T(2,128)(2,1)} %reshape.77), calls=%async_computation | async-start | bytes 262144 | tf_op jit(solution)/shard_map/all_to_all | solution.py:17
  29.6 6.8 %copy.60 = bf16[1,64,8192]{1,0,2:T(2,128)(2,1)} copy(bf16[1,64,8192]{2,1,0:T(8,128)(2,1)S(1)} %copy-done.1) | data formatting | bytes 2097152 | tf_op args[0]
  36.4 45.3 %reduce.2 = bf16[8192,64]{1,0:T(8,128)(2,1)S(1)} reduce(bf16[8192,1,64]{2,1,0:T(2,128)(2,1)} %bitcast.88, bf16[]{:T(256)} %broadcast.103), dimensions={1}, to_apply=%bitcast.64.reduce_sub_computation | reduce | bytes 2097154
  81.7 2.7 reshape.79
  85.0 5.9 %all-to-all-start.2 = ((bf16[8,2,32768]{2,1,0:T(2,128)(2,1)}), bf16[8,2,32768]{2,1,0:T(2,128)(2,1)S(1)}, u32[]{:S(2)}, u32[]{:S(2)}) async-start(bf16[8,2,32768]{2,1,0:T(2,128)(2,1)} %reshape.79), calls=%async_computation.2 | async-start | bytes 2097152 | tf_op jit(solution)/shard_map/all_to_all | solution.py:16
  95.5 20.1 %all-to-all-done.2 = bf16[8,2,32768]{2,1,0:T(2,128)(2,1)S(1)} async-done(((bf16[8,2,32768]{2,1,0:T(2,128)(2,1)}), bf16[8,2,32768]{2,1,0:T(2,128)(2,1)S(1)}, u32[]{:S(2)}, u32[]{:S(2)}) %all-to-all-start.2) | async-done | bytes 1048608 | tf_op jit(solution)/shard_map/all_to_all | solution.py:16
  115.6 4.3 %reshape.80 = bf16[8192,1,64]{2,1,0:T(2,128)(2,1)} reshape(bf16[8,2,32768]{2,1,0:T(2,128)(2,1)S(1)} %all-to-all-done.2) | data formatting | bytes 2097152
  119.9 8.2 %copy.61 = bf16[1,64,8192]{2,1,0:T(8,128)(2,1)S(1)} copy(bf16[1,64,8192]{1,0,2:T(2,128)(2,1)} %bitcast.87) | data formatting | bytes 2097152 | tf_op jit(solution)/shard_map/all_to_all | solution.py:16
  129.6 109.2 %conditional.1 = (f32[8,512]{1,0:T(8,128)}, f32[8,512,128]{1,2,0:T(8,128)}) conditional(s32[]{:T(128)} %convert_element_type.20, () %tuple.17, (bf16[2,2048,128]{2,1,0:T(8,128)(2,1)}, s32[512]{0:T(512)S(1)}, s32[4]{0:T(128)S(1)}, s32[]{:T(128)}, s32[512]{0:T(512)S(1)}, /*index=5*/bf16[8,512,128]{2,0,1:T(8,128)(2,1)S(1)}) %tuple.52), branch_computations={%region_3.4_spmd, %region_4.10_spmd} | conditional | flops 560029696 | bytes 36120976 | solution.py:70
  131.2 107.6 %while.12 = (s32[]{:T(128)}, f32[8,512]{1,0:T(8,128)}, f32[8,512,128]{1,2,0:T(8,128)}, s32[8]{0:T(128)S(1)}, bf16[8,512,128]{2,1,0:T(8,128)(2,1)S(1)}, /*index=5...) while((s32[]{:T(128)}, f32[8,512]{1,0:T(8,128)}, ...), condition=%wide.region_9.9_spmd.clone, body=%wide.region_6.8_spmd.clone.sunk | while | flops 560006656 | bytes 31914204 | solution.py:66
  135.3 1.9 copy-done
  140.5 3.4 %fusion.34 = f32[1,512,128]{2,1,0:T(8,128)S(1)} fusion(f32[512,2048]{1,0:T(8,128)} %copy-done, s32[512]{0:T(512)S(1)} %get-tuple-element.264, s32[2048]{0:T(1024)S(1)} %get-tuple-element.262, f32[512]{0:T(512)S(1)} %broadcast_maximum_fusion.2, s32[512]{0:T(512)S(1)} %get-tuple-element.263, bf16[2048,1,128]{2,0,1:T(8,128)(2,1)S(1)} %get-tuple-element.261, ...), kind=kOutput, calls=%fused_computation.10.clone.1 | convolution fusion | flops 276889600 | bytes 4997120 | tf_op jit(solution)/shard_map/cond/branch_1_fun/while/body/eval_jaxpr/dot_general | solution.py:61
  148.8 1.9 copy-done
  153.9 3.4 %fusion.34 = f32[1,512,128]{2,1,0:T(8,128)S(1)} fusion(f32[512,2048]{1,0:T(8,128)} %copy-done, s32[512]{0:T(512)S(1)} %get-tuple-element.264, s32[2048]{0:T(1024)S(1)} %get-tuple-element.262, f32[512]{0:T(512)S(1)} %broadcast_maximum_fusion.2, s32[512]{0:T(512)S(1)} %get-tuple-element.263, bf16[2048,1,128]{2,0,1:T(8,128)(2,1)S(1)} %get-tuple-element.261, ...), kind=kOutput, calls=%fused_computation.10.clone.1 | convolution fusion | flops 276889600 | bytes 4997120 | tf_op jit(solution)/shard_map/cond/branch_1_fun/while/body/eval_jaxpr/dot_general | solution.py:61
  162.2 1.9 copy-done
  167.3 3.4 %fusion.34 = f32[1,512,128]{2,1,0:T(8,128)S(1)} fusion(f32[512,2048]{1,0:T(8,128)} %copy-done, s32[512]{0:T(512)S(1)} %get-tuple-element.264, s32[2048]{0:T(1024)S(1)} %get-tuple-element.262, f32[512]{0:T(512)S(1)} %broadcast_maximum_fusion.2, s32[512]{0:T(512)S(1)} %get-tuple-element.263, bf16[2048,1,128]{2,0,1:T(8,128)(2,1)S(1)} %get-tuple-element.261, ...), kind=kOutput, calls=%fused_computation.10.clone.1 | convolution fusion | flops 276889600 | bytes 4997120 | tf_op jit(solution)/shard_map/cond/branch_1_fun/while/body/eval_jaxpr/dot_general | solution.py:61
  175.7 1.9 copy-done
  180.8 3.4 %fusion.34 = f32[1,512,128]{2,1,0:T(8,128)S(1)} fusion(f32[512,2048]{1,0:T(8,128)} %copy-done, s32[512]{0:T(512)S(1)} %get-tuple-element.264, s32[2048]{0:T(1024)S(1)} %get-tuple-element.262, f32[512]{0:T(512)S(1)} %broadcast_maximum_fusion.2, s32[512]{0:T(512)S(1)} %get-tuple-element.263, bf16[2048,1,128]{2,0,1:T(8,128)(2,1)S(1)} %get-tuple-element.261, ...), kind=kOutput, calls=%fused_computation.10.clone.1 | convolution fusion | flops 276889600 | bytes 4997120 | tf_op jit(solution)/shard_map/cond/branch_1_fun/while/body/eval_jaxpr/dot_general | solution.py:61
  189.2 1.9 copy-done
  194.3 3.4 %fusion.34 = f32[1,512,128]{2,1,0:T(8,128)S(1)} fusion(f32[512,2048]{1,0:T(8,128)} %copy-done, s32[512]{0:T(512)S(1)} %get-tuple-element.264, s32[2048]{0:T(1024)S(1)} %get-tuple-element.262, f32[512]{0:T(512)S(1)} %broadcast_maximum_fusion.2, s32[512]{0:T(512)S(1)} %get-tuple-element.263, bf16[2048,1,128]{2,0,1:T(8,128)(2,1)S(1)} %get-tuple-element.261, ...), kind=kOutput, calls=%fused_computation.10.clone.1 | convolution fusion | flops 276889600 | bytes 4997120 | tf_op jit(solution)/shard_map/cond/branch_1_fun/while/body/eval_jaxpr/dot_general | solution.py:61
  207.7 3.4 %fusion.34 = f32[1,512,128]{2,1,0:T(8,128)S(1)} fusion(f32[512,2048]{1,0:T(8,128)} %copy-done, s32[512]{0:T(512)S(1)} %get-tuple-element.264, s32[2048]{0:T(1024)S(1)} %get-tuple-element.262, f32[512]{0:T(512)S(1)} %broadcast_maximum_fusion.2, s32[512]{0:T(512)S(1)} %get-tuple-element.263, bf16[2048,1,128]{2,0,1:T(8,128)(2,1)S(1)} %get-tuple-element.261, ...), kind=kOutput, calls=%fused_computation.10.clone.1 | convolution fusion | flops 276889600 | bytes 4997120 | tf_op jit(solution)/shard_map/cond/branch_1_fun/while/body/eval_jaxpr/dot_general | solution.py:61
  216.1 1.9 copy-done
  221.2 3.4 %fusion.34 = f32[1,512,128]{2,1,0:T(8,128)S(1)} fusion(f32[512,2048]{1,0:T(8,128)} %copy-done, s32[512]{0:T(512)S(1)} %get-tuple-element.264, s32[2048]{0:T(1024)S(1)} %get-tuple-element.262, f32[512]{0:T(512)S(1)} %broadcast_maximum_fusion.2, s32[512]{0:T(512)S(1)} %get-tuple-element.263, bf16[2048,1,128]{2,0,1:T(8,128)(2,1)S(1)} %get-tuple-element.261, ...), kind=kOutput, calls=%fused_computation.10.clone.1 | convolution fusion | flops 276889600 | bytes 4997120 | tf_op jit(solution)/shard_map/cond/branch_1_fun/while/body/eval_jaxpr/dot_general | solution.py:61
  229.5 1.9 copy-done
  234.6 3.4 %fusion.34 = f32[1,512,128]{2,1,0:T(8,128)S(1)} fusion(f32[512,2048]{1,0:T(8,128)} %copy-done, s32[512]{0:T(512)S(1)} %get-tuple-element.264, s32[2048]{0:T(1024)S(1)} %get-tuple-element.262, f32[512]{0:T(512)S(1)} %broadcast_maximum_fusion.2, s32[512]{0:T(512)S(1)} %get-tuple-element.263, bf16[2048,1,128]{2,0,1:T(8,128)(2,1)S(1)} %get-tuple-element.261, ...), kind=kOutput, calls=%fused_computation.10.clone.1 | convolution fusion | flops 276889600 | bytes 4997120 | tf_op jit(solution)/shard_map/cond/branch_1_fun/while/body/eval_jaxpr/dot_general | solution.py:61
  240.7 2.0 copy.65
  242.7 6.8 %reduce.3 = bf16[512,1024]{1,0:T(8,128)(2,1)S(1)} reduce(bf16[512,1,1024]{2,1,0:T(2,128)(2,1)S(1)} %bitcast.90, bf16[]{:T(256)} %broadcast.103), dimensions={1}, to_apply=%bitcast.66.reduce_sub_computation | reduce | bytes 2097154
  250.4 29.1 %all_to_all.69 = bf16[8,2,32768]{2,1,0:T(2,128)(2,1)S(1)} all-to-all(bf16[8,2,32768]{2,1,0:T(2,128)(2,1)S(1)} %reshape.81), channel_id=1, replica_groups=mesh['parts'=1,'uly'=8,'blk'=4] {'uly'}, dimensions={0} | all-to-all | bytes 2097152 | tf_op jit(solution)/shard_map/all_to_all | solution.py:73
  (120 shorter events, 67.3 us)
Async XLA Ops:
  6.5 23.1 %copy-start.1 = (bf16[1,64,8192]{2,1,0:T(8,128)(2,1)S(1)}, bf16[1,64,8192]{2,1,0:T(8,128)(2,1)}, u32[]{:S(2)}) copy-start(bf16[1,64,8192]{2,1,0:T(8,128)(2,1)} %param.8) | copy-start | bytes 3145732
  11.6 14.6 %all-to-all-start.1 = ((bf16[8,2,4096]{2,1,0:T(2,128)(2,1)}), bf16[8,2,4096]{2,1,0:T(2,128)(2,1)S(1)}, u32[]{:S(2)}, u32[]{:S(2)}) async-start(bf16[8,2,4096]{2,1,0:T(2,128)(2,1)} %reshape.75), calls=%async_computation.1 | async-start | bytes 262144 | tf_op jit(solution)/shard_map/all_to_all | solution.py:18
  26.2 58.8 %all-to-all-start = ((bf16[8,2,4096]{2,1,0:T(2,128)(2,1)}), bf16[8,2,4096]{2,1,0:T(2,128)(2,1)S(1)}, u32[]{:S(2)}, u32[]{:S(2)}) async-start(bf16[8,2,4096]{2,1,0:T(2,128)(2,1)} %reshape.77), calls=%async_computation | async-start | bytes 262144 | tf_op jit(solution)/shard_map/all_to_all | solution.py:17
  84.4 8.4 %copy-start.2 = (s32[4]{0:T(128)S(1)}, s32[4]{0:T(128)}, u32[]{:S(2)}) copy-start(s32[4]{0:T(128)} %param.11) | copy-start | bytes 52
  85.0 30.5 %all-to-all-start.2 = ((bf16[8,2,32768]{2,1,0:T(2,128)(2,1)}), bf16[8,2,32768]{2,1,0:T(2,128)(2,1)S(1)}, u32[]{:S(2)}, u32[]{:S(2)}) async-start(bf16[8,2,32768]{2,1,0:T(2,128)(2,1)} %reshape.79), calls=%async_computation.2 | async-start | bytes 2097152 | tf_op jit(solution)/shard_map/all_to_all | solution.py:16
  91.0 38.7 %all-gather.2.cloned.1.call-start = ((), (), s32[]{:S(2)}) async-start(), calls=%async_computation.4 | async-start | bytes 1310720 | tf_op jit(solution)/shard_map/all_gather | solution.py:41
  135.3 1.9 copy-start
  148.8 1.9 copy-start
  162.2 1.9 copy-start
  175.7 1.9 copy-start
  189.1 1.9 copy-start
  202.6 1.9 copy-start
  216.1 1.9 copy-start
  229.5 1.9 copy-start
Sparse Core Ops, SparseCore 0:
  93.3 18.1 all-gather.1
where the time goes:
time: 290 us; the launch traced here: 289 us
  local copies, waits for them, and re-layouts  75.2 us (26%)
  other arithmetic  75 us (26%)
  matrix products  37.7 us (13%)
  blocking collectives  29.1 us (10%)
  waiting for transfers between devices  23.1 us (8%)
  loops' own time  17 us (6%)
  starting transfers between devices  16.7 us (6%)
  between operations  14.9 us (5%)
    unnamed x4, other arithmetic  56.7 us
    all_to_all x1, blocking collectives, on_device(): lax.all_to_all(outputs, 'uly', split_axis=1, concat_axis=2, tiled=True)  29.1 us
    dot_general x8, matrix products, one_head(): jnp.dot(expo.astype(jnp.bfloat16), vh, preferred_element_type=jnp.float32)  26.9 us
    unnamed x21, local copies, waits for them, and re-layouts  22.4 us
    all_to_all x1, waiting for transfers between devices, on_device(): lax.all_to_all(queries, 'uly', split_axis=2, concat_axis=1, tiled=True)  20.1 us
    dynamic_update_slice x24, local copies, waits for them, and re-layouts, work(): lax.map(one_head, (jnp.arange(local_q, dtype=jnp.int32),) + tuple(state))  17.6 us
    another operation x1, loops' own time, work(): lax.map(one_head, (jnp.arange(local_q, dtype=jnp.int32),) + tuple(state))  16.9 us
    while x16, local copies, waits for them, and re-layouts  15.3 us
  transfers between devices with their start and end apart: 4, of which 2 were waited for; matrix products, arithmetic and copies ran while one was open for 27% of the time, Pallas kernels for 0%

commit v1 on v0

--- a/solution.py
+++ b/solution.py
@@ -1,17 +1,24 @@
+import functools
+import math
+
 import jax
 import jax.numpy as jnp
 from jax import lax
+from jax.experimental import pallas as pl
+from jax.experimental.pallas import tpu as pltpu
 from jax.sharding import PartitionSpec as P
 
 HEAD_WIDTH = 128
 BLOCK = 128
+FAR = 1e30
+RATE = math.log2(math.e) / math.sqrt(HEAD_WIDTH)
 
 
 def segment_of(positions, ends):
     return jnp.sum((positions[:, None] >= ends[None, :]).astype(jnp.int32), axis=1)
 
 
-def on_device(queries, keys, values, doc_blocks):
+def general(queries, keys, values, doc_blocks):
     moved_q, moved_k, moved_v = (
         lax.all_to_all(queries, "uly", split_axis=2, concat_axis=1, tiled=True),
         lax.all_to_all(keys, "uly", split_axis=2, concat_axis=1, tiled=True),
@@ -73,7 +80,136 @@
     return lax.all_to_all(outputs, "uly", split_axis=1, concat_axis=2, tiled=True)
 
 
+def segment_starts(doc_blocks, positions):
+    ends = jnp.cumsum(doc_blocks) * BLOCK
+    return jnp.max(jnp.where(ends[None, :] <= positions[:, None], ends[None, :], 0), axis=1)
+
+
+def spread(doc_blocks, slices, share, slot):
+    first = lax.axis_index("uly") * share + jnp.arange(slices, dtype=jnp.int32) * slot
+    return segment_starts(doc_blocks, first)
+
+
+def update(q_ref, kv_ref, starts_ref, most, total, accum, g, other, me, dims, first):
+    slices, share, group, kv_heads, slot = dims
+    width = HEAD_WIDTH
+    for b in range(slices):
+        rows = [
+            q_ref[b, :, pl.ds(pl.multiple_of((g * group + h) * width, width), width)]
+            for h in range(group)
+        ]
+        q = jnp.concatenate(rows, axis=0)
+        count = (b + 1) * share
+        k = kv_ref[other, 0:count, pl.ds(pl.multiple_of(g * width, width), width)]
+        v = kv_ref[other, 0:count, pl.ds(pl.multiple_of((kv_heads + g) * width, width), width)]
+        scores = lax.dot_general(
+            k, q, (((1,), (1,)), ((), ())), preferred_element_type=jnp.float32
+        )
+        start = starts_ref[b]
+        parts, penalties, tops = [], [], []
+        for c in range(b + 1):
+            part = scores[c * share:(c + 1) * share]
+            if first and c == b:
+                token = lax.broadcasted_iota(jnp.int32, part.shape, 1) % share
+                key = lax.broadcasted_iota(jnp.int32, part.shape, 0)
+                part = jnp.where(key <= token, part, -FAR)
+                penalty = jnp.float32(0)
+            else:
+                allowed = c * slot + other * share >= start
+                if c == b:
+                    allowed = allowed & (other < me)
+                penalty = jnp.where(allowed, jnp.float32(0), jnp.float32(FAR))
+            parts.append(part)
+            penalties.append(penalty)
+            tops.append(jnp.max(part, axis=0, keepdims=True) - penalty)
+        top = functools.reduce(jnp.maximum, tops)
+        if not first:
+            old = most[g, b]
+            top = jnp.maximum(top, old)
+        scaled = top * RATE
+        weights = [
+            jnp.exp2(part * RATE - (scaled + penalty)) for part, penalty in zip(parts, penalties)
+        ]
+        summed = functools.reduce(
+            jnp.add, [jnp.sum(weight, axis=0, keepdims=True) for weight in weights]
+        )
+        weights = jnp.concatenate([weight.astype(jnp.bfloat16) for weight in weights], axis=0)
+        product = lax.dot_general(
+            v, weights, (((0,), (0,)), ((), ())), preferred_element_type=jnp.float32
+        )
+        most[g, b] = top
+        if first:
+            total[g, b] = summed
+            accum[g, b] = product
+        else:
+            factor = jnp.exp2((old - top) * RATE)
+            total[g, b] = total[g, b] * factor + summed
+            accum[g, b] = accum[g, b] * factor + product
+
+
+def finish(out_ref, total, accum, g, dims):
+    slices, share, group, kv_heads, slot = dims
+    width = HEAD_WIDTH
+    for b in range(slices):
+        done = (accum[g, b] / total[g, b]).T.astype(jnp.bfloat16)
+        for h in range(group):
+            out_ref[b, :, pl.ds(pl.multiple_of((g * group + h) * width, width), width)] = done[
+                h * share:(h + 1) * share
+            ]
+
+
+def attend(dims, n_uly, q_ref, kv_ref, starts_ref, out_ref, most, total, accum):
+    me = lax.axis_index("uly")
+    kv_heads = dims[3]
+
+    @pl.loop(0, kv_heads)
+    def _(g):
+        update(q_ref, kv_ref, starts_ref, most, total, accum, g, me, me, dims, True)
+
+        @pl.loop(1, n_uly)
+        def _(step):
+            other = lax.rem(me + step, n_uly)
+            update(q_ref, kv_ref, starts_ref, most, total, accum, g, other, me, dims, False)
+
+        finish(out_ref, total, accum, g, dims)
+
+
+def by_heads(queries, keys, values, doc_blocks, n_uly, n_blk):
+    share = queries.shape[1]
+    slot = share * n_uly
+    swap = lambda x: lax.all_to_all(x, "blk", split_axis=2, concat_axis=0, tiled=True)
+    kv = jnp.concatenate([swap(keys), swap(values)], axis=2)
+    kv = lax.all_gather(kv.reshape(n_blk * share, kv.shape[2]), "uly", axis=0)
+    q = swap(queries)
+    kv_heads = kv.shape[2] // (2 * HEAD_WIDTH)
+    group = q.shape[2] // HEAD_WIDTH // kv_heads
+    dims = (n_blk, share, group, kv_heads, slot)
+    starts = spread(doc_blocks, n_blk, share, slot)
+    vmem = pl.BlockSpec(memory_space=pltpu.VMEM)
+    rows = group * share
+    out = pl.pallas_call(
+        functools.partial(attend, dims, n_uly),
+        out_shape=jax.ShapeDtypeStruct(q.shape, jnp.bfloat16),
+        in_specs=[vmem, vmem, pl.BlockSpec(memory_space=pltpu.SMEM)],
+        out_specs=vmem,
+        scratch_shapes=[
+            pltpu.VMEM((kv_heads, n_blk, 1, rows), jnp.float32),
+            pltpu.VMEM((kv_heads, n_blk, 1, rows), jnp.float32),
+            pltpu.VMEM((kv_heads, n_blk, HEAD_WIDTH, rows), jnp.float32),
+        ],
+        compiler_params=pltpu.CompilerParams(vmem_limit_bytes=40 * 1024 * 1024),
+    )(q, kv, starts)
+    return lax.all_to_all(out, "blk", split_axis=0, concat_axis=2, tiled=True)
+
+
 def solution(mesh):
+    n_uly, n_blk = mesh.shape["uly"], mesh.shape["blk"]
+
+    def on_device(queries, keys, values, doc_blocks):
+        if (keys.shape[2] // HEAD_WIDTH) % n_blk == 0:
+            return by_heads(queries, keys, values, doc_blocks, n_uly, n_blk)
+        return general(queries, keys, values, doc_blocks)
+
     return jax.shard_map(
         on_device,
         mesh=mesh,

time: 290 us -> 158 us (0.54)
  local copies, waits for them, and re-layouts: 75.2 us -> 23.9 us
  matrix products: 37.7 us -> 0 us
  other arithmetic: 75 us -> 50.8 us
  Pallas kernels: 0 us -> 22.1 us
  loops' own time: 17 us -> 0 us
  blocking collectives: 29.1 us -> 16.9 us
  starting transfers between devices: 16.7 us -> 11.3 us
  waiting for transfers between devices: 23.1 us -> 18.8 us
    dot_general x16 -> x0, matrix products: 37.7 us -> none  [the longest x8 26.9 us: one_head(): jnp.dot(expo.astype(jnp.bfloat16), vh, preferred_element_type=jnp.float32)]
    pallas_call x0 -> x1, Pallas kernels: none -> 22.1 us  [by_heads(): pl.pallas_call(functools.partial(attend, dims, n_uly), out_shape=jax.Shap...]
    dynamic_update_slice x24 -> x0, local copies, waits for them, and re-layouts: 17.6 us -> none  [work(): lax.map(one_head, (jnp.arange(local_q, dtype=jnp.int32),) + tuple(state))]
    another operation x2 -> x0, loops' own time: 17 us -> none  [the longest x1 16.9 us: work(): lax.map(one_head, (jnp.arange(local_q, dtype=jnp.int32),) + tuple(state))]
    reduce_sum x11 -> x0, other arithmetic: 15.4 us -> none  [the longest x8 14.6 us: one_head(): summed = summed * factor + jnp.sum(expo, axis=1)]
    while x16 -> x0, local copies, waits for them, and re-layouts: 15.3 us -> none
    all_to_all x1, blocking collectives: 29.1 us -> 16.9 us  [by_heads(): return lax.all_to_all(out, 'blk', split_axis=0, concat_axis=2, tiled=True)]
    all_to_all x10 -> x8, local copies, waits for them, and re-layouts: 10.6 us -> 2.7 us  [the longest x7 1.66 us: by_heads(): lax.all_to_all(x, 'blk', split_axis=2, concat_axis=0, tiled=True)]
  transfers between devices with their start and end apart: 4 -> 4, of which waited for: 2 -> 3; matrix products, arithmetic and copies ran while one was open for 27% -> 42% of each run, Pallas kernels for 0% -> 0%
where the time goes in v1:
time: 158 us; the launch traced here: 157 us
  other arithmetic  50.8 us (32%)
  local copies, waits for them, and re-layouts  23.9 us (15%)
  Pallas kernels  22.1 us (14%)
  waiting for transfers between devices  18.8 us (12%)
  blocking collectives  16.9 us (11%)
  between operations  13.6 us (9%)
  starting transfers between devices  11.3 us (7%)
    unnamed x3, other arithmetic  49.7 us
    pallas_call x1, Pallas kernels, by_heads(): pl.pallas_call(functools.partial(attend, dims, n_uly), out_shape=jax.Shap...  22.1 us
    unnamed x19, local copies, waits for them, and re-layouts  21.2 us
    all_to_all x3, waiting for transfers between devices, by_heads(): lax.all_to_all(x, 'blk', split_axis=2, concat_axis=0, tiled=True)  18.7 us
    all_to_all x1, blocking collectives, by_heads(): return lax.all_to_all(out, 'blk', split_axis=0, concat_axis=2, tiled=True)  16.9 us
    all_to_all x3, starting transfers between devices, by_heads(): lax.all_to_all(x, 'blk', split_axis=2, concat_axis=0, tiled=True)  11.3 us
  transfers between devices with their start and end apart: 4, of which 3 were waited for; matrix products, arithmetic and copies ran while one was open for 42% of the time, Pallas kernels for 0%

profile of v1, /device:TPU:0, one launch (start us, length us, event | category | flops | bytes accessed | tf_op | source)
XLA Modules:
  0.0 157.4 jit_solution(4545435692762243401)
XLA Ops:
  6.5 1.2 copy.43
  7.8 0.5 broadcast.24
  8.3 2.3 %reduce.1 = bf16[1024,64]{1,0:T(8,128)(2,1)S(1)} reduce(bf16[1024,1,64]{2,1,0:T(2,128)(2,1)S(1)} %bitcast.29, bf16[]{:T(256)} %broadcast.24), dimensions={1}, to_apply=%bitcast.18.reduce_sub_computation | reduce | bytes 262146
  10.6 0.9 reshape.40
  11.5 4.2 %all-to-all-start.2 = ((bf16[4,2,8192]{2,1,0:T(2,128)(2,1)}), bf16[4,2,8192]{2,1,0:T(2,128)(2,1)S(1)}, u32[]{:S(2)}, u32[]{:S(2)}) async-start(bf16[4,2,8192]{2,1,0:T(2,128)(2,1)} %reshape.40), calls=%async_computation.2 | async-start | bytes 262144 | tf_op jit(solution)/shard_map/all_to_all | solution.py:180
  15.7 0.4 copy.40
  16.1 2.3 %reduce.2 = bf16[1024,64]{1,0:T(8,128)(2,1)S(1)} reduce(bf16[1024,1,64]{2,1,0:T(2,128)(2,1)S(1)} %bitcast.30, bf16[]{:T(256)} %broadcast.24), dimensions={1}, to_apply=%bitcast.20.reduce_sub_computation | reduce | bytes 262146
  18.4 0.9 reshape.42
  19.3 1.1 all-to-all-done.2
  20.4 3.3 %all-to-all-start.1 = ((bf16[4,2,8192]{2,1,0:T(2,128)(2,1)}), bf16[4,2,8192]{2,1,0:T(2,128)(2,1)S(1)}, u32[]{:S(2)}, u32[]{:S(2)}) async-start(bf16[4,2,8192]{2,1,0:T(2,128)(2,1)} %reshape.42), calls=%async_computation.1 | async-start | bytes 262144 | tf_op jit(solution)/shard_map/all_to_all | solution.py:180
  23.7 0.3 reshape.41
  24.1 0.3 copy.44
  24.4 0.1 all_to_all.56
  24.5 3.8 %all-to-all-done.1 = bf16[4,2,8192]{2,1,0:T(2,128)(2,1)S(1)} async-done(((bf16[4,2,8192]{2,1,0:T(2,128)(2,1)}), bf16[4,2,8192]{2,1,0:T(2,128)(2,1)S(1)}, u32[]{:S(2)}, u32[]{:S(2)}) %all-to-all-start.1) | async-done | bytes 131104 | tf_op jit(solution)/shard_map/all_to_all | solution.py:180
  28.3 0.3 reshape.43
  28.6 0.3 copy.41
  28.9 0.1 all_to_all.53
  29.0 0.7 pad_maximum_fusion
  29.8 6.8 %copy.37 = bf16[1,64,8192]{1,0,2:T(2,128)(2,1)} copy(bf16[1,64,8192]{2,1,0:T(8,128)(2,1)S(1)} %copy-done.1) | data formatting | bytes 2097152 | tf_op args[0]
  36.6 45.2 %reduce = bf16[8192,64]{1,0:T(8,128)(2,1)S(1)} reduce(bf16[8192,1,64]{2,1,0:T(2,128)(2,1)} %bitcast.23, bf16[]{:T(256)} %broadcast.24), dimensions={1}, to_apply=%bitcast.16.reduce_sub_computation | reduce | bytes 2097154
  81.8 2.7 %reshape.38 = bf16[4,2,65536]{2,1,0:T(2,128)(2,1)} reshape(bf16[8192,64]{1,0:T(8,128)(2,1)S(1)} %reduce) | data formatting | bytes 2097152
  84.5 3.7 %all-to-all-start = ((bf16[4,2,65536]{2,1,0:T(2,128)(2,1)}), bf16[4,2,65536]{2,1,0:T(2,128)(2,1)S(1)}, u32[]{:S(2)}, u32[]{:S(2)}) async-start(bf16[4,2,65536]{2,1,0:T(2,128)(2,1)} %reshape.38), calls=%async_computation | async-start | bytes 2097152 | tf_op jit(solution)/shard_map/all_to_all | solution.py:180
  88.2 0.2 reduce-window.8
  88.4 0.2 select_reduce_fusion.starts_ref
  88.6 13.9 %all-to-all-done = bf16[4,2,65536]{2,1,0:T(2,128)(2,1)S(1)} async-done(((bf16[4,2,65536]{2,1,0:T(2,128)(2,1)}), bf16[4,2,65536]{2,1,0:T(2,128)(2,1)S(1)}, u32[]{:S(2)}, u32[]{:S(2)}) %all-to-all-start) | async-done | bytes 1048608 | tf_op jit(solution)/shard_map/all_to_all | solution.py:180
  102.5 3.1 %reshape.39 = bf16[8192,1,64]{2,1,0:T(2,128)(2,1)} reshape(bf16[4,2,65536]{2,1,0:T(2,128)(2,1)S(1)} %all-to-all-done) | data formatting | bytes 2097152
  105.6 2.5 %copy.49 = bf16[1,64,8192]{1,2,0:T(8,128)(2,1)S(1)} copy(bf16[1,64,8192]{1,0,2:T(2,128)(2,1)} %bitcast.24) | data formatting | bytes 2097152
  108.0 0.8 copy.39
  108.9 1.6 %copy-done = bf16[8,256,512]{2,1,0:T(8,128)(2,1)S(1)} copy-done((bf16[8,256,512]{2,1,0:T(8,128)(2,1)S(1)}, bf16[8,256,512]{2,1,0:T(8,128)(2,1)}, u32[]{:S(2)}) %copy-start) | copy-done | bytes 2097176
  110.5 22.1 %shard_map.46 = bf16[4,64,2048]{2,1,0:T(8,128)(2,1)S(1)} custom-call(bf16[4,64,2048]{2,1,0:T(8,128)(2,1)S(1)} %bitcast.22, bf16[8,256,512]{2,1,0:T(8,128)(2,1)S(1)} %copy-done, s32[4]{0:T(128)S(1)} %select_reduce_fusion.starts_ref), custom_call_target="tpu_custom_call" | custom-call | tf_op jit(solution)/shard_map/pallas_call | solution.py:190
  132.6 16.9 %all_to_all.66 = bf16[4,64,2048]{2,1,0:T(8,128)(2,1)S(1)} all-to-all(bf16[4,64,2048]{2,1,0:T(8,128)(2,1)S(1)} %shard_map.46), channel_id=1, replica_groups=mesh['parts'=1,'uly'=8,'blk'=4] {'blk'}, dimensions={0} | all-to-all | bytes 2097152 | tf_op jit(solution)/shard_map/all_to_all | solution.py:202
  149.5 1.0 copy.50
  (14 shorter events, 0.1 us)
Async XLA Ops:
  6.5 9.2 %copy-start.2 = (bf16[1,64,1024]{2,1,0:T(8,128)(2,1)S(1)}, bf16[1,64,1024]{2,1,0:T(8,128)(2,1)}, u32[]{:S(2)}) copy-start(bf16[1,64,1024]{2,1,0:T(8,128)(2,1)} %param.5) | copy-start | bytes 393220
  11.5 8.9 %all-to-all-start.2 = ((bf16[4,2,8192]{2,1,0:T(2,128)(2,1)}), bf16[4,2,8192]{2,1,0:T(2,128)(2,1)S(1)}, u32[]{:S(2)}, u32[]{:S(2)}) async-start(bf16[4,2,8192]{2,1,0:T(2,128)(2,1)} %reshape.40), calls=%async_computation.2 | async-start | bytes 262144 | tf_op jit(solution)/shard_map/all_to_all | solution.py:180
  20.4 7.9 %all-to-all-start.1 = ((bf16[4,2,8192]{2,1,0:T(2,128)(2,1)}), bf16[4,2,8192]{2,1,0:T(2,128)(2,1)S(1)}, u32[]{:S(2)}, u32[]{:S(2)}) async-start(bf16[4,2,8192]{2,1,0:T(2,128)(2,1)} %reshape.42), calls=%async_computation.1 | async-start | bytes 262144 | tf_op jit(solution)/shard_map/all_to_all | solution.py:180
  23.7 6.1 %copy-start.1 = (bf16[1,64,8192]{2,1,0:T(8,128)(2,1)S(1)}, bf16[1,64,8192]{2,1,0:T(8,128)(2,1)}, u32[]{:S(2)}) copy-start(bf16[1,64,8192]{2,1,0:T(8,128)(2,1)} %param.4) | copy-start | bytes 3145732
  23.7 85.2 %all-gather.2.cloned.1.call-start = ((), (), s32[]{:S(2)}) async-start(), calls=%async_computation.4 | async-start | bytes 2359296 | tf_op jit(solution)/shard_map/all_gather | solution.py:182
  81.8 6.4 %copy-start.3 = (s32[4]{0:T(128)S(1)}, s32[4]{0:T(128)}, u32[]{:S(2)}) copy-start(s32[4]{0:T(128)} %param.7) | copy-start | bytes 52
  84.5 18.0 %all-to-all-start = ((bf16[4,2,65536]{2,1,0:T(2,128)(2,1)}), bf16[4,2,65536]{2,1,0:T(2,128)(2,1)S(1)}, u32[]{:S(2)}, u32[]{:S(2)}) async-start(bf16[4,2,65536]{2,1,0:T(2,128)(2,1)} %reshape.38), calls=%async_computation | async-start | bytes 2097152 | tf_op jit(solution)/shard_map/all_to_all | solution.py:180
  108.9 1.6 %copy-start = (bf16[8,256,512]{2,1,0:T(8,128)(2,1)S(1)}, bf16[8,256,512]{2,1,0:T(8,128)(2,1)}, u32[]{:S(2)}) copy-start(bf16[8,256,512]{2,1,0:T(8,128)(2,1)} %all-gather.2.cloned.1.call-done.kv_ref) | copy-start | bytes 6291460
Sparse Core Ops, SparseCore 0:
  29.9 50.0 all-gather.1

commit v2 on v0

--- a/solution.py
+++ b/solution.py
@@ -1,17 +1,24 @@
+import functools
+import math
+
 import jax
 import jax.numpy as jnp
 from jax import lax
+from jax.experimental import pallas as pl
+from jax.experimental.pallas import tpu as pltpu
 from jax.sharding import PartitionSpec as P
 
 HEAD_WIDTH = 128
 BLOCK = 128
+FAR = 1e30
+RATE = math.log2(math.e) / math.sqrt(HEAD_WIDTH)
 
 
 def segment_of(positions, ends):
     return jnp.sum((positions[:, None] >= ends[None, :]).astype(jnp.int32), axis=1)
 
 
-def on_device(queries, keys, values, doc_blocks):
+def general(queries, keys, values, doc_blocks):
     moved_q, moved_k, moved_v = (
         lax.all_to_all(queries, "uly", split_axis=2, concat_axis=1, tiled=True),
         lax.all_to_all(keys, "uly", split_axis=2, concat_axis=1, tiled=True),
@@ -73,7 +80,285 @@
     return lax.all_to_all(outputs, "uly", split_axis=1, concat_axis=2, tiled=True)
 
 
+MESH = pl.DeviceIdType.MESH
+
+
+def ring_place(device, columns):
+    row, side = device // 2, device % 2
+    return side * (2 * columns - 1 - row) + (1 - side) * row
+
+
+def ring_device(place, columns):
+    back = place // columns
+    return back * ((2 * columns - 1 - place) * 2 + 1) + (1 - back) * (place * 2)
+
+
+def update(q_buf, kv_buf, starts, state, g, others, me, dims, blocks, first):
+    slices, share, group, slot = dims
+    most, total, accum = state
+    for b in blocks:
+        q = jnp.concatenate(
+            [q_buf[g, b, :, h * HEAD_WIDTH:(h + 1) * HEAD_WIDTH] for h in range(group)], axis=0
+        )
+        count = (b + 1) * share
+        parts, penalties, tops = [], [], []
+        for other in others:
+            scores = lax.dot_general(
+                kv_buf[0, g, other, 0:count, :], q, (((1,), (1,)), ((), ())),
+                preferred_element_type=jnp.float32,
+            )
+            for c in range(b + 1):
+                part = scores[c * share:(c + 1) * share]
+                if first and c == b:
+                    token = lax.broadcasted_iota(jnp.int32, part.shape, 1) % share
+                    key = lax.broadcasted_iota(jnp.int32, part.shape, 0)
+                    part = jnp.where(key <= token, part, -FAR)
+                    penalty = jnp.float32(0)
+                else:
+                    allowed = c * slot + other * share >= starts[b]
+                    if c == b:
+                        allowed = jnp.logical_and(allowed, other < me)
+                    penalty = jnp.where(allowed, jnp.float32(0), jnp.float32(FAR))
+                parts.append(part)
+                penalties.append(penalty)
+                tops.append(jnp.max(part, axis=0, keepdims=True) - penalty)
+        top = functools.reduce(jnp.maximum, tops)
+        if not first:
+            old = most[g, b]
+            top = jnp.maximum(top, old)
+        scaled = top * RATE
+        weights = [
+            jnp.exp2(part * RATE - (scaled + penalty)) for part, penalty in zip(parts, penalties)
+        ]
+        summed = jnp.sum(functools.reduce(jnp.add, weights), axis=0, keepdims=True)
+        weights = [weight.astype(jnp.bfloat16) for weight in weights]
+        products = [
+            lax.dot_general(
+                kv_buf[1, g, other, 0:count, :],
+                jnp.concatenate(weights[i * (b + 1):(i + 1) * (b + 1)], axis=0),
+                (((0,), (0,)), ((), ())), preferred_element_type=jnp.float32,
+            )
+            for i, other in enumerate(others)
+        ]
+        product = functools.reduce(jnp.add, products)
+        most[g, b] = top
+        if first:
+            total[g, b] = summed
+            accum[g, b] = product
+        else:
+            factor = jnp.exp2((old - top) * RATE)
+            total[g, b] = total[g, b] * factor + summed
+            accum[g, b] = accum[g, b] * factor + product
+
+
+def attend(
+    dims, n_uly, kv_heads, docs, q_ref, k_ref, v_ref, docs_ref, out_ref,
+    q_buf, kv_buf, o_buf, most, total, accum,
+    swap_send, swap_recv, q_send, q_recv, ring_send, ring_recv, o_send, o_recv,
+):
+    slices, share, group, slot = dims
+    width = HEAD_WIDTH
+    half = n_uly // 2
+    me, block = lax.axis_index("uly"), lax.axis_index("blk")
+    place = ring_place(me, half)
+    at = lambda offset: ring_device(lax.rem(place + offset + n_uly, n_uly), half)
+    ahead, behind = at(1), at(-1)
+    state = (most, total, accum)
+    wide = group * width
+
+    barrier = pltpu.get_barrier_semaphore()
+    for other in (ahead, behind):
+        pl.semaphore_signal(barrier, inc=1, device_id={"uly": other}, device_id_type=MESH)
+    for d in range(1, slices):
+        peer = lax.rem(block + d, slices)
+        pl.semaphore_signal(barrier, inc=1, device_id={"blk": peer}, device_id_type=MESH)
+    pl.semaphore_wait(barrier, slices + 1)
+
+    def rows(b):
+        return pl.ds(pl.multiple_of(b * share, share), share)
+
+    def columns(start, size):
+        return pl.ds(pl.multiple_of(start, width), size)
+
+    def swap_copy(part, g, d):
+        peer = lax.rem(block + d, slices)
+        return pltpu.make_async_remote_copy(
+            src_ref=(k_ref, v_ref)[part].at[:, columns((peer * kv_heads + g) * width, width)],
+            dst_ref=kv_buf.at[part, g, me, rows(block), :],
+            send_sem=swap_send.at[part, g, d - 1],
+            recv_sem=swap_recv.at[part, g, d - 1],
+            device_id={"blk": peer},
+            device_id_type=MESH,
+        )
+
+    def q_copy(g, d):
+        peer = lax.rem(block + d, slices)
+        return pltpu.make_async_remote_copy(
+            src_ref=q_ref.at[:, columns((peer * kv_heads + g) * wide, wide)],
+            dst_ref=q_buf.at[g, block],
+            send_sem=q_send.at[g, d - 1],
+            recv_sem=q_recv.at[g, d - 1],
+            device_id={"blk": peer},
+            device_id_type=MESH,
+        )
+
+    def o_copy(g, d):
+        peer = lax.rem(block + d, slices)
+        return pltpu.make_async_remote_copy(
+            src_ref=o_buf.at[g, peer],
+            dst_ref=out_ref.at[:, columns((block * kv_heads + g) * wide, wide)],
+            send_sem=o_send.at[g, d - 1],
+            recv_sem=o_recv.at[g, d - 1],
+            device_id={"blk": peer},
+            device_id_type=MESH,
+        )
+
+    def ring_copy(part, way, g, hop):
+        origin = at(-hop) if way == 0 else at(hop)
+        tile = kv_buf.at[part, g, origin]
+        return pltpu.make_async_remote_copy(
+            src_ref=tile,
+            dst_ref=tile,
+            send_sem=ring_send.at[part, way, g, hop],
+            recv_sem=ring_recv.at[part, way, g, hop],
+            device_id={"uly": ahead if way == 0 else behind},
+            device_id_type=MESH,
+        )
+
+    def swap_wait(part, g):
+        for d in range(1, slices):
+            swap_copy(part, g, d).wait_recv()
+
+    def hops(way, g):
+        return half if way == g % 2 else half - 1
+
+    def poll(part, g, s):
+        if s == half - 2 and g + 1 < kv_heads:
+            swap_wait(part, g + 1)
+        for way in range(2):
+            if s > hops(way, g):
+                continue
+            ring_copy(part, way, g, s - 1).wait_recv()
+            if s < hops(way, g):
+                ring_copy(part, way, g, s).start()
+            if s == hops(way, g) - 1 and g + 1 < kv_heads:
+                ring_copy(part, way, g + 1, 0).start()
+
+    for g in range(kv_heads):
+        for part in range(2):
+            for d in range(1, slices):
+                swap_copy(part, g, d).start()
+        for d in range(1, slices):
+            q_copy(g, d).start()
+    for g in range(kv_heads):
+        for part in range(2):
+            kv_buf[part, g, me, rows(block), :] = (k_ref, v_ref)[part][
+                :, columns((block * kv_heads + g) * width, width)
+            ]
+        q_buf[g, block] = q_ref[:, columns((block * kv_heads + g) * wide, wide)]
+    for part in range(2):
+        swap_wait(part, 0)
+        for way in range(2):
+            ring_copy(part, way, 0, 0).start()
+
+    ends, so_far = [], 0
+    for d in range(docs):
+        so_far = so_far + docs_ref[d] * BLOCK
+        ends.append(so_far)
+    starts = []
+    for b in range(slices):
+        position = b * slot + me * share
+        start = jnp.int32(0)
+        for end in ends:
+            start = jnp.where(end <= position, end, start)
+        starts.append(start)
+
+    every = range(slices)
+    early, late = [b for b in every if b % 4 in (0, 3)], [b for b in every if b % 4 in (1, 2)]
+    poll(0, 0, 1)
+    poll(1, 0, 1)
+    for g in range(kv_heads):
+        for d in range(1, slices):
+            q_copy(g, d).wait_recv()
+        update(q_buf, kv_buf, starts, state, g, [me], me, dims, every, True)
+        for s in range(1, half + 1):
+            if s < half:
+                others = [at(-s), at(s)]
+            else:
+                others = [at(half)]
+            after = (g, s + 1) if s < half else (g + 1, 1)
+            update(q_buf, kv_buf, starts, state, g, others, me, dims, early, False)
+            if after[0] < kv_heads:
+                poll(0, *after)
+            update(q_buf, kv_buf, starts, state, g, others, me, dims, late, False)
+            if after[0] < kv_heads:
+                poll(1, *after)
+        for b in every:
+            done = (accum[g, b] / total[g, b]).T.astype(jnp.bfloat16)
+            for h in range(group):
+                o_buf[g, b, :, h * width:(h + 1) * width] = done[h * share:(h + 1) * share]
+        for d in range(1, slices):
+            o_copy(g, d).start()
+        out_ref[:, columns((block * kv_heads + g) * wide, wide)] = o_buf[g, block]
+    for g in range(kv_heads):
+        for d in range(1, slices):
+            for part in range(2):
+                swap_copy(part, g, d).wait_send()
+            q_copy(g, d).wait_send()
+        for part in range(2):
+            for way in range(2):
+                for hop in range(hops(way, g)):
+                    ring_copy(part, way, g, hop).wait_send()
+        for d in range(1, slices):
+            o_copy(g, d).wait()
+
+
+def by_heads(queries, keys, values, doc_blocks, n_uly, n_blk):
+    share = queries.shape[1]
+    slot = share * n_uly
+    kv_heads = keys.shape[2] // HEAD_WIDTH // n_blk
+    group = queries.shape[2] // keys.shape[2]
+    docs = doc_blocks.shape[0]
+    dims = (n_blk, share, group, slot)
+    vmem = pl.BlockSpec(memory_space=pltpu.VMEM)
+    rows, wide, half = group * share, group * HEAD_WIDTH, n_uly // 2
+    dma = pltpu.SemaphoreType.DMA
+    out = pl.pallas_call(
+        functools.partial(attend, dims, n_uly, kv_heads, docs),
+        out_shape=jax.ShapeDtypeStruct(queries.shape[1:], jnp.bfloat16),
+        in_specs=[vmem, vmem, vmem, pl.BlockSpec(memory_space=pltpu.SMEM)],
+        out_specs=vmem,
+        scratch_shapes=[
+            pltpu.VMEM((kv_heads, n_blk, share, wide), jnp.bfloat16),
+            pltpu.VMEM((2, kv_heads, n_uly, n_blk * share, HEAD_WIDTH), jnp.bfloat16),
+            pltpu.VMEM((kv_heads, n_blk, share, wide), jnp.bfloat16),
+            pltpu.VMEM((kv_heads, n_blk, 1, rows), jnp.float32),
+            pltpu.VMEM((kv_heads, n_blk, 1, rows), jnp.float32),
+            pltpu.VMEM((kv_heads, n_blk, HEAD_WIDTH, rows), jnp.float32),
+            dma((2, kv_heads, n_blk - 1)),
+            dma((2, kv_heads, n_blk - 1)),
+            dma((kv_heads, n_blk - 1)),
+            dma((kv_heads, n_blk - 1)),
+            dma((2, 2, kv_heads, half)),
+            dma((2, 2, kv_heads, half)),
+            dma((kv_heads, n_blk - 1)),
+            dma((kv_heads, n_blk - 1)),
+        ],
+        compiler_params=pltpu.CompilerParams(
+            collective_id=0, has_side_effects=True, vmem_limit_bytes=48 * 1024 * 1024
+        ),
+    )(queries[0], keys[0], values[0], doc_blocks)
+    return out[None]
+
+
 def solution(mesh):
+    n_uly, n_blk = mesh.shape["uly"], mesh.shape["blk"]
+
+    def on_device(queries, keys, values, doc_blocks):
+        if (keys.shape[2] // HEAD_WIDTH) % n_blk == 0 and n_uly % 2 == 0 and n_uly > 4:
+            return by_heads(queries, keys, values, doc_blocks, n_uly, n_blk)
+        return general(queries, keys, values, doc_blocks)
+
     return jax.shard_map(
         on_device,
         mesh=mesh,

time: 290 us -> 51.9 us (0.18)
  other arithmetic: 75 us -> 0 us
  local copies, waits for them, and re-layouts: 75.2 us -> 4.66 us
  Pallas kernels: 0 us -> 47 us
  matrix products: 37.7 us -> 0 us
  blocking collectives: 29.1 us -> 0 us
  waiting for transfers between devices: 23.1 us -> 0 us
  loops' own time: 17 us -> 0 us
  starting transfers between devices: 16.7 us -> 0 us
  between operations: 14.9 us -> 0.01 us
    unnamed x4 -> x0, other arithmetic: 56.7 us -> none
    pallas_call x0 -> x1, Pallas kernels: none -> 47 us  [by_heads(): pl.pallas_call(functools.partial(attend, dims, n_uly, kv_heads, docs), ou...]
    dot_general x16 -> x0, matrix products: 37.7 us -> none  [the longest x8 26.9 us: one_head(): jnp.dot(expo.astype(jnp.bfloat16), vh, preferred_element_type=jnp.float32)]
    all_to_all x1 -> x0, blocking collectives: 29.1 us -> none  [on_device(): lax.all_to_all(outputs, 'uly', split_axis=1, concat_axis=2, tiled=True)]
    all_to_all x3 -> x0, waiting for transfers between devices: 23 us -> none  [the longest x1 20.1 us: on_device(): lax.all_to_all(queries, 'uly', split_axis=2, concat_axis=1, tiled=True)]
    unnamed x21 -> x9, local copies, waits for them, and re-layouts: 22.4 us -> 4.66 us
    dynamic_update_slice x24 -> x0, local copies, waits for them, and re-layouts: 17.6 us -> none  [work(): lax.map(one_head, (jnp.arange(local_q, dtype=jnp.int32),) + tuple(state))]
    another operation x2 -> x0, loops' own time: 17 us -> none  [the longest x1 16.9 us: work(): lax.map(one_head, (jnp.arange(local_q, dtype=jnp.int32),) + tuple(state))]
  transfers between devices with their start and end apart: 4 -> 0, of which waited for: 2 -> 0; matrix products, arithmetic and copies ran while one was open for 27% -> 0% of each run, Pallas kernels for 0% -> 0%
where the time goes in v2:
time: 51.9 us; the launch traced here: 51.7 us
  Pallas kernels  47 us (91%)
  local copies, waits for them, and re-layouts  4.66 us (9%)
    pallas_call x1, Pallas kernels, by_heads(): pl.pallas_call(functools.partial(attend, dims, n_uly, kv_heads, docs), ou...  47 us
    unnamed x9, local copies, waits for them, and re-layouts  4.66 us

profile of v2, /device:TPU:0, one launch (start us, length us, event | category | flops | bytes accessed | tf_op | source)
XLA Modules:
  0.0 51.7 jit_solution(13674810994719213616)
XLA Ops:
  0.0 0.0 copy-start.3
  0.0 0.7 %copy-done.3 = s32[4]{0:T(128)S(1)} copy-done((s32[4]{0:T(128)S(1)}, s32[4]{0:T(128)}, u32[]{:S(2)}) %copy-start.3) | copy-done | bytes 40
  0.7 0.0 copy-start
  0.7 1.2 %copy-done = bf16[1,64,8192]{2,1,0:T(8,128)(2,1)S(1)} copy-done((bf16[1,64,8192]{2,1,0:T(8,128)(2,1)S(1)}, bf16[1,64,8192]{2,1,0:T(8,128)(2,1)}, u32[]{:S(2)}) %copy-start) | copy-done | bytes 1048600
  1.9 0.0 copy-start.1
  1.9 0.9 %copy-done.1 = bf16[1,64,1024]{2,1,0:T(8,128)(2,1)S(1)} copy-done((bf16[1,64,1024]{2,1,0:T(8,128)(2,1)S(1)}, bf16[1,64,1024]{2,1,0:T(8,128)(2,1)}, u32[]{:S(2)}) %copy-start.1) | copy-done | bytes 131096
  2.8 0.0 copy-start.2
  2.8 0.9 %copy-done.2 = bf16[1,64,1024]{2,1,0:T(8,128)(2,1)S(1)} copy-done((bf16[1,64,1024]{2,1,0:T(8,128)(2,1)S(1)}, bf16[1,64,1024]{2,1,0:T(8,128)(2,1)}, u32[]{:S(2)}) %copy-start.2) | copy-done | bytes 131096
  3.7 47.0 %shard_map.46 = bf16[64,8192]{1,0:T(8,128)(2,1)S(1)} custom-call(bf16[64,8192]{1,0:T(8,128)(2,1)S(1)} %bitcast.5, bf16[64,1024]{1,0:T(8,128)(2,1)S(1)} %bitcast.6, bf16[64,1024]{1,0:T(8,128)(2,1)S(1)} %bitcast.7, s32[4]{0:T(128)S(1)} %copy-done.3), custom_call_target="tpu_custom_call" | custom-call | tf_op jit(solution)/shard_map/pallas_call | solution.py:326
  50.7 1.0 %copy.6 = bf16[1,64,8192]{2,1,0:T(8,128)(2,1)} copy(bf16[1,64,8192]{2,1,0:T(8,128)(2,1)S(1)} %bitcast.4) | data formatting | bytes 2097152
Async XLA Ops:
  0.0 0.7 %copy-start.3 = (s32[4]{0:T(128)S(1)}, s32[4]{0:T(128)}, u32[]{:S(2)}) copy-start(s32[4]{0:T(128)} %docs_ref.1) | copy-start | bytes 52
  0.7 1.2 %copy-start = (bf16[1,64,8192]{2,1,0:T(8,128)(2,1)S(1)}, bf16[1,64,8192]{2,1,0:T(8,128)(2,1)}, u32[]{:S(2)}) copy-start(bf16[1,64,8192]{2,1,0:T(8,128)(2,1)} %param.4) | copy-start | bytes 3145732
  1.9 0.9 %copy-start.1 = (bf16[1,64,1024]{2,1,0:T(8,128)(2,1)S(1)}, bf16[1,64,1024]{2,1,0:T(8,128)(2,1)}, u32[]{:S(2)}) copy-start(bf16[1,64,1024]{2,1,0:T(8,128)(2,1)} %param.5) | copy-start | bytes 393220
  2.8 0.9 %copy-start.2 = (bf16[1,64,1024]{2,1,0:T(8,128)(2,1)S(1)}, bf16[1,64,1024]{2,1,0:T(8,128)(2,1)}, u32[]{:S(2)}) copy-start(bf16[1,64,1024]{2,1,0:T(8,128)(2,1)} %param.6) | copy-start | bytes 393220

commit v3 on v2

--- a/solution.py
+++ b/solution.py
@@ -101,46 +101,36 @@
             [q_buf[g, b, :, h * HEAD_WIDTH:(h + 1) * HEAD_WIDTH] for h in range(group)], axis=0
         )
         count = (b + 1) * share
-        parts, penalties, tops = [], [], []
-        for other in others:
-            scores = lax.dot_general(
-                kv_buf[0, g, other, 0:count, :], q, (((1,), (1,)), ((), ())),
-                preferred_element_type=jnp.float32,
-            )
-            for c in range(b + 1):
-                part = scores[c * share:(c + 1) * share]
-                if first and c == b:
-                    token = lax.broadcasted_iota(jnp.int32, part.shape, 1) % share
-                    key = lax.broadcasted_iota(jnp.int32, part.shape, 0)
-                    part = jnp.where(key <= token, part, -FAR)
-                    penalty = jnp.float32(0)
-                else:
-                    allowed = c * slot + other * share >= starts[b]
-                    if c == b:
-                        allowed = jnp.logical_and(allowed, other < me)
-                    penalty = jnp.where(allowed, jnp.float32(0), jnp.float32(FAR))
-                parts.append(part)
-                penalties.append(penalty)
-                tops.append(jnp.max(part, axis=0, keepdims=True) - penalty)
-        top = functools.reduce(jnp.maximum, tops)
+        while count * len(others) % HEAD_WIDTH:
+            count += share
+        k = jnp.concatenate([kv_buf[0, g, other, 0:count, :] for other in others], axis=0)
+        v = jnp.concatenate([kv_buf[1, g, other, 0:count, :] for other in others], axis=0)
+        scores = lax.dot_general(
+            q, k, (((1,), (1,)), ((), ())), preferred_element_type=jnp.float32
+        )
+        size = k.shape[0]
+        token = b * slot + me * share
+        lane = lax.broadcasted_iota(jnp.int32, (1, size), 1)
+        index = lane % count
+        origin = jnp.where(lane < count, others[0], others[-1])
+        key = (index // share) * slot + index % share + origin * share
+        allowed = key >= starts[b]
+        if first:
+            row = lax.broadcasted_iota(jnp.int32, scores.shape, 0) % share
+            scores = jnp.where(jnp.logical_and(allowed, key <= token + row), scores, -FAR)
+        else:
+            allowed = jnp.logical_and(allowed, key < token)
+            scores = scores + jnp.where(allowed, jnp.float32(0), jnp.float32(-FAR))
+        tiles = [scores[:, i:i + HEAD_WIDTH] for i in range(0, size, HEAD_WIDTH)]
+        top = jnp.max(functools.reduce(jnp.maximum, tiles), axis=1, keepdims=True)
+        top = jnp.broadcast_to(top, (scores.shape[0], HEAD_WIDTH))
         if not first:
             old = most[g, b]
             top = jnp.maximum(top, old)
-        scaled = top * RATE
-        weights = [
-            jnp.exp2(part * RATE - (scaled + penalty)) for part, penalty in zip(parts, penalties)
-        ]
-        summed = jnp.sum(functools.reduce(jnp.add, weights), axis=0, keepdims=True)
-        weights = [weight.astype(jnp.bfloat16) for weight in weights]
-        products = [
-            lax.dot_general(
-                kv_buf[1, g, other, 0:count, :],
-                jnp.concatenate(weights[i * (b + 1):(i + 1) * (b + 1)], axis=0),
-                (((0,), (0,)), ((), ())), preferred_element_type=jnp.float32,
-            )
-            for i, other in enumerate(others)
-        ]
-        product = functools.reduce(jnp.add, products)
+        weights = [jnp.exp2((tile - top) * RATE) for tile in tiles]
+        summed = functools.reduce(jnp.add, weights)
+        weights = jnp.concatenate([weight.astype(jnp.bfloat16) for weight in weights], axis=1)
+        product = jnp.dot(weights, v, preferred_element_type=jnp.float32)
         most[g, b] = top
         if first:
             total[g, b] = summed
@@ -154,7 +144,7 @@
 def attend(
     dims, n_uly, kv_heads, docs, q_ref, k_ref, v_ref, docs_ref, out_ref,
     q_buf, kv_buf, o_buf, most, total, accum,
-    swap_send, swap_recv, q_send, q_recv, ring_send, ring_recv, o_send, o_recv,
+    swap_send, swap_recv, q_send, q_recv, ring_send, ring_recv, o_send, o_recv, own_kv, own_q,
 ):
     slices, share, group, slot = dims
     width = HEAD_WIDTH
@@ -166,6 +156,31 @@
     state = (most, total, accum)
     wide = group * width
 
+    def rows(b):
+        return pl.ds(pl.multiple_of(b * share, share), share)
+
+    def columns(start, size):
+        return pl.ds(pl.multiple_of(start, width), size)
+
+    def own_kv_copy(part, g):
+        return pltpu.make_async_copy(
+            (k_ref, v_ref)[part].at[:, columns((block * kv_heads + g) * width, width)],
+            kv_buf.at[part, g, me, rows(block), :],
+            own_kv.at[part, g],
+        )
+
+    def own_q_copy(g):
+        return pltpu.make_async_copy(
+            q_ref.at[:, columns((block * kv_heads + g) * wide, wide)],
+            q_buf.at[g, block],
+            own_q.at[g],
+        )
+
+    for g in range(kv_heads):
+        for part in range(2):
+            own_kv_copy(part, g).start()
+        own_q_copy(g).start()
+
     barrier = pltpu.get_barrier_semaphore()
     for other in (ahead, behind):
         pl.semaphore_signal(barrier, inc=1, device_id={"uly": other}, device_id_type=MESH)
@@ -173,12 +188,6 @@
         peer = lax.rem(block + d, slices)
         pl.semaphore_signal(barrier, inc=1, device_id={"blk": peer}, device_id_type=MESH)
     pl.semaphore_wait(barrier, slices + 1)
-
-    def rows(b):
-        return pl.ds(pl.multiple_of(b * share, share), share)
-
-    def columns(start, size):
-        return pl.ds(pl.multiple_of(start, width), size)
 
     def swap_copy(part, g, d):
         peer = lax.rem(block + d, slices)
@@ -202,8 +211,8 @@
             device_id_type=MESH,
         )
 
-    def o_copy(g, d):
-        peer = lax.rem(block + d, slices)
+    def o_copy(g, peer):
+        d = lax.rem(peer - block + slices, slices)
         return pltpu.make_async_remote_copy(
             src_ref=o_buf.at[g, peer],
             dst_ref=out_ref.at[:, columns((block * kv_heads + g) * wide, wide)],
@@ -226,6 +235,7 @@
         )
 
     def swap_wait(part, g):
+        own_kv_copy(part, g).wait()
         for d in range(1, slices):
             swap_copy(part, g, d).wait_recv()
 
@@ -250,12 +260,6 @@
                 swap_copy(part, g, d).start()
         for d in range(1, slices):
             q_copy(g, d).start()
-    for g in range(kv_heads):
-        for part in range(2):
-            kv_buf[part, g, me, rows(block), :] = (k_ref, v_ref)[part][
-                :, columns((block * kv_heads + g) * width, width)
-            ]
-        q_buf[g, block] = q_ref[:, columns((block * kv_heads + g) * wide, wide)]
     for part in range(2):
         swap_wait(part, 0)
         for way in range(2):
@@ -280,6 +284,7 @@
     for g in range(kv_heads):
         for d in range(1, slices):
             q_copy(g, d).wait_recv()
+        own_q_copy(g).wait()
         update(q_buf, kv_buf, starts, state, g, [me], me, dims, every, True)
         for s in range(1, half + 1):
             if s < half:
@@ -287,18 +292,19 @@
             else:
                 others = [at(half)]
             after = (g, s + 1) if s < half else (g + 1, 1)
-            update(q_buf, kv_buf, starts, state, g, others, me, dims, early, False)
-            if after[0] < kv_heads:
-                poll(0, *after)
-            update(q_buf, kv_buf, starts, state, g, others, me, dims, late, False)
-            if after[0] < kv_heads:
-                poll(1, *after)
-        for b in every:
-            done = (accum[g, b] / total[g, b]).T.astype(jnp.bfloat16)
-            for h in range(group):
-                o_buf[g, b, :, h * width:(h + 1) * width] = done[h * share:(h + 1) * share]
-        for d in range(1, slices):
-            o_copy(g, d).start()
+            for part, blocks in enumerate((early, late)):
+                for b in blocks:
+                    update(q_buf, kv_buf, starts, state, g, others, me, dims, [b], False)
+                    if s == half:
+                        done = accum[g, b] / jnp.sum(total[g, b], axis=1, keepdims=True)
+                        done = done.astype(jnp.bfloat16)
+                        for h in range(group):
+                            o_buf[g, b, :, h * width:(h + 1) * width] = done[
+                                h * share:(h + 1) * share
+                            ]
+                        pl.when(b != block)(lambda b=b: o_copy(g, b).start())
+                if after[0] < kv_heads:
+                    poll(part, *after)
         out_ref[:, columns((block * kv_heads + g) * wide, wide)] = o_buf[g, block]
     for g in range(kv_heads):
         for d in range(1, slices):
@@ -310,7 +316,7 @@
                 for hop in range(hops(way, g)):
                     ring_copy(part, way, g, hop).wait_send()
         for d in range(1, slices):
-            o_copy(g, d).wait()
+            o_copy(g, lax.rem(block + d, slices)).wait()
 
 
 def by_heads(queries, keys, values, doc_blocks, n_uly, n_blk):
@@ -321,20 +327,21 @@
     docs = doc_blocks.shape[0]
     dims = (n_blk, share, group, slot)
     vmem = pl.BlockSpec(memory_space=pltpu.VMEM)
+    anywhere = pl.BlockSpec(memory_space=pl.ANY)
     rows, wide, half = group * share, group * HEAD_WIDTH, n_uly // 2
     dma = pltpu.SemaphoreType.DMA
     out = pl.pallas_call(
         functools.partial(attend, dims, n_uly, kv_heads, docs),
         out_shape=jax.ShapeDtypeStruct(queries.shape[1:], jnp.bfloat16),
-        in_specs=[vmem, vmem, vmem, pl.BlockSpec(memory_space=pltpu.SMEM)],
+        in_specs=[anywhere, anywhere, anywhere, pl.BlockSpec(memory_space=pltpu.SMEM)],
         out_specs=vmem,
         scratch_shapes=[
             pltpu.VMEM((kv_heads, n_blk, share, wide), jnp.bfloat16),
             pltpu.VMEM((2, kv_heads, n_uly, n_blk * share, HEAD_WIDTH), jnp.bfloat16),
             pltpu.VMEM((kv_heads, n_blk, share, wide), jnp.bfloat16),
-            pltpu.VMEM((kv_heads, n_blk, 1, rows), jnp.float32),
-            pltpu.VMEM((kv_heads, n_blk, 1, rows), jnp.float32),
-            pltpu.VMEM((kv_heads, n_blk, HEAD_WIDTH, rows), jnp.float32),
+            pltpu.VMEM((kv_heads, n_blk, rows, HEAD_WIDTH), jnp.float32),
+            pltpu.VMEM((kv_heads, n_blk, rows, HEAD_WIDTH), jnp.float32),
+            pltpu.VMEM((kv_heads, n_blk, rows, HEAD_WIDTH), jnp.float32),
             dma((2, kv_heads, n_blk - 1)),
             dma((2, kv_heads, n_blk - 1)),
             dma((kv_heads, n_blk - 1)),
@@ -343,9 +350,11 @@
             dma((2, 2, kv_heads, half)),
             dma((kv_heads, n_blk - 1)),
             dma((kv_heads, n_blk - 1)),
+            dma((2, kv_heads)),
+            dma((kv_heads,)),
         ],
         compiler_params=pltpu.CompilerParams(
-            collective_id=0, has_side_effects=True, vmem_limit_bytes=48 * 1024 * 1024
+            collective_id=0, has_side_effects=True, vmem_limit_bytes=60 * 1024 * 1024
         ),
     )(queries[0], keys[0], values[0], doc_blocks)
     return out[None]

time: 51.9 us -> 48.9 us (0.942)
  local copies, waits for them, and re-layouts: 4.66 us -> 2.26 us
    unnamed x9 -> x1, local copies, waits for them, and re-layouts: 4.66 us -> 2.26 us
where the time goes in v3:
time: 48.9 us; the launch traced here: 48.8 us
  Pallas kernels  46.5 us (95%)
  local copies, waits for them, and re-layouts  2.26 us (5%)
    pallas_call x1, Pallas kernels, by_heads(): pl.pallas_call(functools.partial(attend, dims, n_uly, kv_heads, docs), ou...  46.5 us
    unnamed x1, local copies, waits for them, and re-layouts  2.26 us

profile of v3, /device:TPU:0, one launch (start us, length us, event | category | flops | bytes accessed | tf_op | source)
XLA Modules:
  0.0 48.8 jit_solution(9616958119013140519)
XLA Ops:
  0.0 46.5 %shard_map.46 = bf16[64,8192]{1,0:T(8,128)(2,1)} custom-call(bf16[64,8192]{1,0:T(8,128)(2,1)} %bitcast.5, bf16[64,1024]{1,0:T(8,128)(2,1)} %bitcast.6, bf16[64,1024]{1,0:T(8,128)(2,1)} %bitcast.7, s32[4]{0:T(128)} %docs_ref.1), custom_call_target="tpu_custom_call" | custom-call | tf_op jit(solution)/shard_map/pallas_call | solution.py:333
  46.5 2.3 %copy.6 = bf16[1,64,8192]{2,1,0:T(8,128)(2,1)} copy(bf16[1,64,8192]{2,1,0:T(8,128)(2,1)} %bitcast.4) | data formatting | bytes 2097152

commit v4 on v3

--- a/solution.py
+++ b/solution.py
@@ -258,12 +258,12 @@
         for part in range(2):
             for d in range(1, slices):
                 swap_copy(part, g, d).start()
-        for d in range(1, slices):
-            q_copy(g, d).start()
     for part in range(2):
         swap_wait(part, 0)
         for way in range(2):
             ring_copy(part, way, 0, 0).start()
+    for d in range(1, slices):
+        q_copy(0, d).start()
 
     ends, so_far = [], 0
     for d in range(docs):
@@ -279,33 +279,39 @@
 
     every = range(slices)
     early, late = [b for b in every if b % 4 in (0, 3)], [b for b in every if b % 4 in (1, 2)]
-    poll(0, 0, 1)
-    poll(1, 0, 1)
-    for g in range(kv_heads):
+    steps = [(g, s) for g in range(kv_heads) for s in range(1, half + 1)]
+    polls = {t: t + 2 for t in range(len(steps) - 3)}
+    for t in range(2):
+        for part in range(2):
+            poll(part, *steps[t])
+    for g in range(1, kv_heads):
         for d in range(1, slices):
-            q_copy(g, d).wait_recv()
-        own_q_copy(g).wait()
-        update(q_buf, kv_buf, starts, state, g, [me], me, dims, every, True)
-        for s in range(1, half + 1):
-            if s < half:
-                others = [at(-s), at(s)]
-            else:
-                others = [at(half)]
-            after = (g, s + 1) if s < half else (g + 1, 1)
-            for part, blocks in enumerate((early, late)):
-                for b in blocks:
-                    update(q_buf, kv_buf, starts, state, g, others, me, dims, [b], False)
-                    if s == half:
-                        done = accum[g, b] / jnp.sum(total[g, b], axis=1, keepdims=True)
-                        done = done.astype(jnp.bfloat16)
-                        for h in range(group):
-                            o_buf[g, b, :, h * width:(h + 1) * width] = done[
-                                h * share:(h + 1) * share
-                            ]
-                        pl.when(b != block)(lambda b=b: o_copy(g, b).start())
-                if after[0] < kv_heads:
-                    poll(part, *after)
-        out_ref[:, columns((block * kv_heads + g) * wide, wide)] = o_buf[g, block]
+            q_copy(g, d).start()
+    for t, (g, s) in enumerate(steps):
+        if s == 1:
+            for d in range(1, slices):
+                q_copy(g, d).wait_recv()
+            own_q_copy(g).wait()
+            update(q_buf, kv_buf, starts, state, g, [me], me, dims, every, True)
+        others = [at(-s), at(s)] if s < half else [at(half)]
+        if t == len(steps) - 1:
+            for part in range(2):
+                poll(part, g, s)
+        for part, blocks in enumerate((early, late)):
+            for b in blocks:
+                update(q_buf, kv_buf, starts, state, g, others, me, dims, [b], False)
+                if s == half:
+                    done = accum[g, b] / jnp.sum(total[g, b], axis=1, keepdims=True)
+                    done = done.astype(jnp.bfloat16)
+                    for h in range(group):
+                        o_buf[g, b, :, h * width:(h + 1) * width] = done[
+                            h * share:(h + 1) * share
+                        ]
+                    pl.when(b != block)(lambda g=g, b=b: o_copy(g, b).start())
+            if t in polls:
+                poll(part, *steps[polls[t]])
+        if s == half:
+            out_ref[:, columns((block * kv_heads + g) * wide, wide)] = o_buf[g, block]
     for g in range(kv_heads):
         for d in range(1, slices):
             for part in range(2):

time: 48.9 us -> 48.4 us (0.990); the launches traced: 48.8 us -> 47.5 us
  Pallas kernels: 46.5 us -> 45.2 us
    pallas_call x1, Pallas kernels: 46.5 us -> 45.2 us  [by_heads(): pl.pallas_call(functools.partial(attend, dims, n_uly, kv_heads, docs), ou...]
where the time goes in v4:
time: 48.4 us; the launch traced here: 47.5 us
  Pallas kernels  45.2 us (93%)
  local copies, waits for them, and re-layouts  2.26 us (5%)
    pallas_call x1, Pallas kernels, by_heads(): pl.pallas_call(functools.partial(attend, dims, n_uly, kv_heads, docs), ou...  45.2 us
    unnamed x1, local copies, waits for them, and re-layouts  2.26 us

profile of v4, /device:TPU:0, one launch (start us, length us, event | category | flops | bytes accessed | tf_op | source)
XLA Modules:
  0.0 47.5 jit_solution(2395700543579990700)
XLA Ops:
  0.0 45.2 %shard_map.46 = bf16[64,8192]{1,0:T(8,128)(2,1)} custom-call(bf16[64,8192]{1,0:T(8,128)(2,1)} %bitcast.5, bf16[64,1024]{1,0:T(8,128)(2,1)} %bitcast.6, bf16[64,1024]{1,0:T(8,128)(2,1)} %bitcast.7, s32[4]{0:T(128)} %docs_ref.1), custom_call_target="tpu_custom_call" | custom-call | tf_op jit(solution)/shard_map/pallas_call | solution.py:339
  45.3 2.3 %copy.6 = bf16[1,64,8192]{2,1,0:T(8,128)(2,1)} copy(bf16[1,64,8192]{2,1,0:T(8,128)(2,1)} %bitcast.4) | data formatting | bytes 2097152

commit v5 on v4

--- a/solution.py
+++ b/solution.py
@@ -93,37 +93,62 @@
     return back * ((2 * columns - 1 - place) * 2 + 1) + (1 - back) * (place * 2)
 
 
-def update(q_buf, kv_buf, starts, state, g, others, me, dims, blocks, first):
+def update(q_buf, kv_buf, starts, state, g, others, me, dims, blocks, first, after=None):
     slices, share, group, slot = dims
     most, total, accum = state
-    for b in blocks:
+    width = HEAD_WIDTH
+
+    def count_of(b):
+        count = (b + 1) * share
+        while count * len(others) % width:
+            count += share
+        return count
+
+    longest = max(count_of(b) for b in blocks)
+    bars = []
+    for other in others:
+        index = lax.broadcasted_iota(jnp.int32, (longest, width), 0)
+        column = lax.broadcasted_iota(jnp.int32, (longest, width), 1)
+        key = (index // share) * slot + index % share + other * share
+        low = jnp.zeros((longest, width), jnp.int32)
+        for b in blocks:
+            low = jnp.where(column == b, starts[b], low)
+        token = column * slot + me * share
+        if first:
+            token = token + share
+        barred = jnp.logical_or(key < low, key >= token)
+        barred = jnp.logical_and(barred, column < slices)
+        bars.append(jnp.where(barred, jnp.float32(-FAR), jnp.float32(0)).astype(jnp.bfloat16))
+
+    def scores_of(b):
         q = jnp.concatenate(
-            [q_buf[g, b, :, h * HEAD_WIDTH:(h + 1) * HEAD_WIDTH] for h in range(group)], axis=0
-        )
-        count = (b + 1) * share
-        while count * len(others) % HEAD_WIDTH:
-            count += share
+            [q_buf[g, b, :, h * width:(h + 1) * width] for h in range(group)], axis=0
+        )
+        pick = lax.broadcasted_iota(jnp.int32, q.shape, 1) == b
+        pick = jnp.where(pick, jnp.float32(1), jnp.float32(0)).astype(jnp.bfloat16)
+        count = count_of(b)
         k = jnp.concatenate([kv_buf[0, g, other, 0:count, :] for other in others], axis=0)
-        v = jnp.concatenate([kv_buf[1, g, other, 0:count, :] for other in others], axis=0)
+        bar = jnp.concatenate([bar[:count] for bar in bars], axis=0)
         scores = lax.dot_general(
-            q, k, (((1,), (1,)), ((), ())), preferred_element_type=jnp.float32
-        )
-        size = k.shape[0]
-        token = b * slot + me * share
-        lane = lax.broadcasted_iota(jnp.int32, (1, size), 1)
-        index = lane % count
-        origin = jnp.where(lane < count, others[0], others[-1])
-        key = (index // share) * slot + index % share + origin * share
-        allowed = key >= starts[b]
+            jnp.concatenate([q, pick], axis=1), jnp.concatenate([k, bar], axis=1),
+            (((1,), (1,)), ((), ())), preferred_element_type=jnp.float32,
+        )
         if first:
             row = lax.broadcasted_iota(jnp.int32, scores.shape, 0) % share
-            scores = jnp.where(jnp.logical_and(allowed, key <= token + row), scores, -FAR)
-        else:
-            allowed = jnp.logical_and(allowed, key < token)
-            scores = scores + jnp.where(allowed, jnp.float32(0), jnp.float32(-FAR))
-        tiles = [scores[:, i:i + HEAD_WIDTH] for i in range(0, size, HEAD_WIDTH)]
+            lane = lax.broadcasted_iota(jnp.int32, scores.shape, 1)
+            scores = jnp.where(lane <= b * share + row, scores, -FAR)
+        return scores
+
+    following = scores_of(blocks[0])
+    for i, b in enumerate(blocks):
+        scores = following
+        if i + 1 < len(blocks):
+            following = scores_of(blocks[i + 1])
+        count = count_of(b)
+        v = jnp.concatenate([kv_buf[1, g, other, 0:count, :] for other in others], axis=0)
+        tiles = [scores[:, i:i + width] for i in range(0, scores.shape[1], width)]
         top = jnp.max(functools.reduce(jnp.maximum, tiles), axis=1, keepdims=True)
-        top = jnp.broadcast_to(top, (scores.shape[0], HEAD_WIDTH))
+        top = jnp.broadcast_to(top, (scores.shape[0], width))
         if not first:
             old = most[g, b]
             top = jnp.maximum(top, old)
@@ -131,14 +156,16 @@
         summed = functools.reduce(jnp.add, weights)
         weights = jnp.concatenate([weight.astype(jnp.bfloat16) for weight in weights], axis=1)
         product = jnp.dot(weights, v, preferred_element_type=jnp.float32)
-        most[g, b] = top
-        if first:
+        if not first:
+            factor = jnp.exp2((old - top) * RATE)
+            summed = total[g, b] * factor + summed
+            product = accum[g, b] * factor + product
+        if after is not None:
+            after(b, summed, product)
+        else:
+            most[g, b] = top
             total[g, b] = summed
             accum[g, b] = product
-        else:
-            factor = jnp.exp2((old - top) * RATE)
-            total[g, b] = total[g, b] * factor + summed
-            accum[g, b] = accum[g, b] * factor + product
 
 
 def attend(
@@ -277,7 +304,7 @@
             start = jnp.where(end <= position, end, start)
         starts.append(start)
 
-    every = range(slices)
+    every = list(range(slices))[::-1]
     early, late = [b for b in every if b % 4 in (0, 3)], [b for b in every if b % 4 in (1, 2)]
     steps = [(g, s) for g in range(kv_heads) for s in range(1, half + 1)]
     polls = {t: t + 2 for t in range(len(steps) - 3)}
@@ -297,18 +324,22 @@
         if t == len(steps) - 1:
             for part in range(2):
                 poll(part, g, s)
-        for part, blocks in enumerate((early, late)):
-            for b in blocks:
-                update(q_buf, kv_buf, starts, state, g, others, me, dims, [b], False)
-                if s == half:
-                    done = accum[g, b] / jnp.sum(total[g, b], axis=1, keepdims=True)
-                    done = done.astype(jnp.bfloat16)
-                    for h in range(group):
-                        o_buf[g, b, :, h * width:(h + 1) * width] = done[
-                            h * share:(h + 1) * share
-                        ]
+
+        def leave(b, summed, product, g=g):
+            done = product / jnp.sum(summed, axis=1, keepdims=True)
+            done = done.astype(jnp.bfloat16)
+            for h in range(group):
+                o_buf[g, b, :, h * width:(h + 1) * width] = done[h * share:(h + 1) * share]
+
+        if s < half:
+            update(q_buf, kv_buf, starts, state, g, others, me, dims, every, False)
+        else:
+            for pair in (early, late):
+                update(q_buf, kv_buf, starts, state, g, others, me, dims, pair, False, leave)
+                for b in pair:
                     pl.when(b != block)(lambda g=g, b=b: o_copy(g, b).start())
-            if t in polls:
+        if t in polls:
+            for part in range(2):
                 poll(part, *steps[polls[t]])
         if s == half:
             out_ref[:, columns((block * kv_heads + g) * wide, wide)] = o_buf[g, block]
@@ -323,6 +354,19 @@
                     ring_copy(part, way, g, hop).wait_send()
         for d in range(1, slices):
             o_copy(g, lax.rem(block + d, slices)).wait()
+
+
+def hand_over(from_ref, to_ref, done):
+    size = from_ref.shape[0] // 4
+    pieces = [pl.ds(i * size, size) for i in range(4)]
+    copies = [
+        pltpu.make_async_copy(from_ref.at[piece], to_ref.at[piece], done.at[i])
+        for i, piece in enumerate(pieces)
+    ]
+    for copy in copies:
+        copy.start()
+    for copy in copies:
+        copy.wait()
 
 
 def by_heads(queries, keys, values, doc_blocks, n_uly, n_blk):
@@ -363,7 +407,14 @@
             collective_id=0, has_side_effects=True, vmem_limit_bytes=60 * 1024 * 1024
         ),
     )(queries[0], keys[0], values[0], doc_blocks)
-    return out[None]
+    return pl.pallas_call(
+        hand_over,
+        out_shape=jax.ShapeDtypeStruct(out.shape, out.dtype),
+        in_specs=[anywhere],
+        out_specs=anywhere,
+        scratch_shapes=[dma((4,))],
+        compiler_params=pltpu.CompilerParams(vmem_limit_bytes=60 * 1024 * 1024),
+    )(out)[None]
 
 
 def solution(mesh):

time: 48.4 us -> 79.5 us (1.64)
  Pallas kernels: 45.2 us -> 78.6 us
  local copies, waits for them, and re-layouts: 2.26 us -> 0 us
    pallas_call x0 -> x1, Pallas kernels: none -> 32.9 us  [by_heads(): pl.pallas_call(hand_over, out_shape=jax.ShapeDtypeStruct(out.shape, out.d...]
    unnamed x1 -> x0, local copies, waits for them, and re-layouts: 2.26 us -> none
where the time goes in v5:
time: 79.5 us; the launch traced here: 78.6 us
  Pallas kernels  78.6 us (99%)
    pallas_call x1, Pallas kernels, by_heads(): pl.pallas_call(functools.partial(attend, dims, n_uly, kv_heads, docs), ou...  45.7 us
    pallas_call x1, Pallas kernels, by_heads(): pl.pallas_call(hand_over, out_shape=jax.ShapeDtypeStruct(out.shape, out.d...  32.9 us

profile of v5, /device:TPU:0, one launch (start us, length us, event | category | flops | bytes accessed | tf_op | source)
XLA Modules:
  0.0 78.6 jit_solution(829059206059422093)
XLA Ops:
  0.0 45.7 %shard_map.46.from_ref = bf16[64,8192]{1,0:T(8,128)(2,1)} custom-call(bf16[64,8192]{1,0:T(8,128)(2,1)} %bitcast.4, bf16[64,1024]{1,0:T(8,128)(2,1)} %bitcast.5, bf16[64,1024]{1,0:T(8,128)(2,1)} %bitcast.6, s32[4]{0:T(128)} %docs_ref.1), custom_call_target="tpu_custom_call" | custom-call | tf_op jit(solution)/shard_map/pallas_call | solution.py:383
  45.7 32.9 %shard_map.47 = bf16[64,8192]{1,0:T(8,128)(2,1)} custom-call(bf16[64,8192]{1,0:T(8,128)(2,1)} %shard_map.46.from_ref), custom_call_target="tpu_custom_call" | custom-call | tf_op jit(solution)/shard_map/pallas_call | solution.py:410

commit v6 on v4

--- a/solution.py
+++ b/solution.py
@@ -325,6 +325,10 @@
             o_copy(g, lax.rem(block + d, slices)).wait()
 
 
+def hand_over(from_ref, to_ref):
+    to_ref[...] = from_ref[...]
+
+
 def by_heads(queries, keys, values, doc_blocks, n_uly, n_blk):
     share = queries.shape[1]
     slot = share * n_uly
@@ -363,7 +367,15 @@
             collective_id=0, has_side_effects=True, vmem_limit_bytes=60 * 1024 * 1024
         ),
     )(queries[0], keys[0], values[0], doc_blocks)
-    return out[None]
+    piece = pl.BlockSpec((out.shape[0] // 4, out.shape[1]), lambda i: (i, 0))
+    return pl.pallas_call(
+        hand_over,
+        grid=(4,),
+        out_shape=jax.ShapeDtypeStruct(out.shape, out.dtype),
+        in_specs=[piece],
+        out_specs=piece,
+        compiler_params=pltpu.CompilerParams(vmem_limit_bytes=60 * 1024 * 1024),
+    )(out)[None]
 
 
 def solution(mesh):

time: 48.4 us -> 49.5 us (1.023)
  Pallas kernels: 45.2 us -> 48.6 us
  local copies, waits for them, and re-layouts: 2.26 us -> 0 us
    pallas_call x0 -> x1, Pallas kernels: none -> 3.37 us  [by_heads(): pl.pallas_call(hand_over, grid=(4,), out_shape=jax.ShapeDtypeStruct(out.s...]
    unnamed x1 -> x0, local copies, waits for them, and re-layouts: 2.26 us -> none
where the time goes in v6:
time: 49.5 us; the launch traced here: 48.6 us
  Pallas kernels  48.6 us (98%)
    pallas_call x1, Pallas kernels, by_heads(): pl.pallas_call(functools.partial(attend, dims, n_uly, kv_heads, docs), ou...  45.2 us
    pallas_call x1, Pallas kernels, by_heads(): pl.pallas_call(hand_over, grid=(4,), out_shape=jax.ShapeDtypeStruct(out.s...  3.37 us

profile of v6, /device:TPU:0, one launch (start us, length us, event | category | flops | bytes accessed | tf_op | source)
XLA Modules:
  0.0 48.6 jit_solution(10771258599011023301)
XLA Ops:
  0.0 45.2 %shard_map.46.from_ref = bf16[64,8192]{1,0:T(8,128)(2,1)} custom-call(bf16[64,8192]{1,0:T(8,128)(2,1)} %bitcast.4, bf16[64,1024]{1,0:T(8,128)(2,1)} %bitcast.5, bf16[64,1024]{1,0:T(8,128)(2,1)} %bitcast.6, s32[4]{0:T(128)} %docs_ref.1), custom_call_target="tpu_custom_call" | custom-call | tf_op jit(solution)/shard_map/pallas_call | solution.py:343
  45.3 3.4 %shard_map.47 = bf16[64,8192]{1,0:T(8,128)(2,1)} custom-call(bf16[64,8192]{1,0:T(8,128)(2,1)} %shard_map.46.from_ref), custom_call_target="tpu_custom_call" | custom-call | tf_op jit(solution)/shard_map/pallas_call | solution.py:371

commit v7 on v4

--- a/solution.py
+++ b/solution.py
@@ -254,16 +254,21 @@
             if s == hops(way, g) - 1 and g + 1 < kv_heads:
                 ring_copy(part, way, g + 1, 0).start()
 
-    for g in range(kv_heads):
-        for part in range(2):
-            for d in range(1, slices):
-                swap_copy(part, g, d).start()
+    for part in range(2):
+        for d in range(1, slices):
+            swap_copy(part, 0, d).start()
+    for d in range(1, slices):
+        q_copy(0, d).start()
     for part in range(2):
         swap_wait(part, 0)
         for way in range(2):
             ring_copy(part, way, 0, 0).start()
-    for d in range(1, slices):
-        q_copy(0, d).start()
+    for g in range(1, kv_heads):
+        for part in range(2):
+            for d in range(1, slices):
+                swap_copy(part, g, d).start()
+        for d in range(1, slices):
+            q_copy(g, d).start()
 
     ends, so_far = [], 0
     for d in range(docs):
@@ -284,9 +289,6 @@
     for t in range(2):
         for part in range(2):
             poll(part, *steps[t])
-    for g in range(1, kv_heads):
-        for d in range(1, slices):
-            q_copy(g, d).start()
     for t, (g, s) in enumerate(steps):
         if s == 1:
             for d in range(1, slices):

time: 48.4 us -> 48.4 us (level)
  Pallas kernels: 45.2 us -> 45.7 us
where the time goes in v7:
time: 48.4 us; the launch traced here: 48 us
  Pallas kernels  45.7 us (94%)
  local copies, waits for them, and re-layouts  2.26 us (5%)
    pallas_call x1, Pallas kernels, by_heads(): pl.pallas_call(functools.partial(attend, dims, n_uly, kv_heads, docs), ou...  45.7 us
    unnamed x1, local copies, waits for them, and re-layouts  2.26 us

profile of v7, /device:TPU:0, one launch (start us, length us, event | category | flops | bytes accessed | tf_op | source)
XLA Modules:
  0.0 48.0 jit_solution(14826418980702313105)
XLA Ops:
  0.0 45.7 %shard_map.46 = bf16[64,8192]{1,0:T(8,128)(2,1)} custom-call(bf16[64,8192]{1,0:T(8,128)(2,1)} %bitcast.5, bf16[64,1024]{1,0:T(8,128)(2,1)} %bitcast.6, bf16[64,1024]{1,0:T(8,128)(2,1)} %bitcast.7, s32[4]{0:T(128)} %docs_ref.1), custom_call_target="tpu_custom_call" | custom-call | tf_op jit(solution)/shard_map/pallas_call | solution.py:341
  45.7 2.3 %copy.6 = bf16[1,64,8192]{2,1,0:T(8,128)(2,1)} copy(bf16[1,64,8192]{2,1,0:T(8,128)(2,1)} %bitcast.4) | data formatting | bytes 2097152
